TPU v7x, 512 devices: a whole 4x8x8 slice. The times are simulated.
512 devices in a mesh: tm: 128 (over z_hi, y, x, core), tmpl: 4 (over z_lo).
Axes of the slice: x: 4, y: 8, z: 8 (z_hi: 2, z_lo: 4; z = z_hi * 4 + z_lo), core: 2. Of those that a mesh axis runs over, the one named last changes fastest.
Arguments:
- records: bfloat16 [1024, 49152], P(None, 'tm'), may hold values from -6 to 6
- templates: bfloat16 [4, 1024, 300], P('tmpl', 'tm'), may hold values from -6 to 6
- shifts: int32 [4, 1024], P('tmpl', 'tm'), may hold values from 0 to 20, as said below
- valid: int32 [4, 1024], P('tmpl', 'tm'), may hold values 0 or 1
Outputs:
- stack: float32 [4, 49152], P('tmpl', 'tm')
Inputs may be any that keep to these rules, and one draw needn't show every extreme that they name: `shifts`: every template has some channel with shift 0 and some channel with shift 20.
All inputs are finite; a program needn't handle non-finite values. No bound on the sum of `valid` on one device may be relied on, other than what follows from the above.
Results may differ from a plain program's by a relative error of at most 0.004.
Values may be sent and summed in bfloat16 or wider, within the bound.
A program may use at most 64 MiB of HBM per device.

v0:
```python
import functools

import jax
import jax.numpy as jnp
from jax import lax
from jax.experimental import pallas as pl
from jax.experimental.pallas import tpu as pltpu
from jax.sharding import PartitionSpec as P

L = 300
MAXS = 20
EPS = 1e-05
KINDS = 4
RING = 8
GROUPS = 16
PIECE = 384
ROWS = 32
OCT = 8
SETS = ROWS // OCT
STEP = 32
SPAN = RING * PIECE
WIDE = SPAN + PIECE
NH = 3584
NZ = 3328
BIG = 3 * 256
LEVELS = 22
BLOCKS = (WIDE // 16)
CHAIN = 208

f32 = jnp.float32
bf16 = jnp.bfloat16


def prepare(message, a_ref):
    pairs = SETS * KINDS * OCT
    low = message[:, :OCT, :].reshape(pairs, 256)
    high = message[:, OCT:, :].reshape(pairs, 256)

    parts = [low[:, :128].astype(bf16), low[:, 128:].astype(bf16), high[:, :128].astype(bf16)]
    lane = lax.broadcasted_iota(jnp.int32, (128, 256), 1)
    line = lax.broadcasted_iota(jnp.int32, (128, 256), 0)
    same = (lane % OCT) == (line % OCT)
    for u_lo in range(4):
        spread = jnp.where(line == STEP * u_lo + lane // OCT, 1.0, 0.0).astype(bf16)
        for u_hi in range(3):
            wide = jnp.dot(parts[u_hi], spread, preferred_element_type=f32)
            block = jnp.where(same, wide, 0.0).astype(bf16)
            for j in range(SETS):
                a_ref[j, 32 * u_lo : 32 * u_lo + 32, 256 * u_hi : 256 * u_hi + 256] = block[32 * j : 32 * j + 32]

    shift = high[:, 128:129]
    valid = high[:, 129:130]
    column = lax.broadcasted_iota(jnp.int32, (pairs, 128), 1)
    squares = low[:, :128] ** 2 + low[:, 128:] ** 2 + high[:, :128] ** 2
    power = jnp.sum(squares, axis=1, keepdims=True) / L
    weight = valid / (L * jnp.sqrt(power + EPS))

    kind = (lax.broadcasted_iota(jnp.int32, (pairs, 128), 0) // OCT) % KINDS
    picked = (shift == (column // KINDS).astype(f32)) & (kind == column % KINDS)
    sel = jnp.transpose(jnp.where(picked, 1.0, 0.0)).astype(bf16)
    return jnp.concatenate([sel, sel], axis=1)[: 4 * LEVELS], weight


def correlate(j, x, h_ref, a_ref, z_ref, corr_ref):
    x8 = jnp.concatenate([x[OCT * j : OCT * j + OCT], jnp.zeros((OCT, NH - WIDE), f32)], axis=1)
    slot = j % 2
    for i in range(STEP // 2):
        first = x8 if i == 0 else pltpu.roll(x8, NH - 2 * i, 1)
        second = pltpu.roll(x8, NH - 2 * i - 1, 1)
        h_ref[slot, 16 * i : 16 * i + 16, :] = jnp.concatenate([first, second], axis=0).astype(bf16)
    for n in range(NZ // 256):
        acc = None
        for u_hi in range(3):
            part = jnp.dot(
                a_ref[j, :, 256 * u_hi : 256 * u_hi + 256],
                h_ref[slot, :, 256 * n + 128 * u_hi : 256 * n + 128 * u_hi + 256],
                preferred_element_type=f32,
            )
            acc = part if acc is None else acc + part
        z_ref[slot, :, 256 * n : 256 * n + 256] = acc
    for k in range(KINDS):
        corr = z_ref[slot, 8 * k : 8 * k + 8, :]
        for u_lo in range(1, 4):
            corr = corr + pltpu.roll(z_ref[slot, 32 * u_lo + 8 * k : 32 * u_lo + 8 * k + 8, :], NZ - STEP * u_lo, 1)
        corr_ref[32 * j + 8 * k : 32 * j + 8 * k + 8, :] = corr


def block_sums(x, run_ref, sum_ref):
    squares = x * x
    quarter = SPAN // 4
    stacked = jnp.concatenate([squares[:, quarter * s : quarter * s + quarter] for s in range(4)], axis=0)
    halo = jnp.concatenate([squares[:, SPAN:], jnp.zeros((128 - ROWS, PIECE), f32)], axis=0)
    for i in range(quarter // 128):
        run_ref[128 * i : 128 * i + 128, :] = jnp.transpose(stacked[:, 128 * i : 128 * i + 128])
    for i in range(PIECE // 128):
        run_ref[quarter + 128 * i : quarter + 128 * i + 128, :] = jnp.transpose(halo[:, 128 * i : 128 * i + 128])
    rows = (quarter + PIECE) // 16
    acc = run_ref[pl.ds(0, rows, stride=16), :]
    for d in range(1, 16):
        acc = acc + run_ref[pl.ds(d, rows, stride=16), :]
        run_ref[pl.ds(d, rows, stride=16), :] = acc
    sum_ref[:rows, :] = acc
    sum_ref[rows:, :] = jnp.zeros((128 - rows, 128), f32)
    final = acc[quarter // 16 - 1 : quarter // 16]
    acc = sum_ref[pl.ds(0, 8, stride=16), :]
    for c in range(1, 16):
        acc = acc + sum_ref[pl.ds(c, 8, stride=16), :]
        sum_ref[pl.ds(c, 8, stride=16), :] = acc
    before = sum_ref[quarter // 16 - 2 : quarter // 16 - 1, :]
    return jnp.concatenate([acc[:3], final, before, jnp.zeros((3, 128), f32)], axis=0)


def window_energy(group, all_ref, run_ref, sum_ref, chain_ref, outer_ref, edge_ref, part_ref):
    for g in range(GROUPS):
        totals = all_ref[g]
        for s in range(4):
            moved = totals if s == 0 else pltpu.roll(totals, 128 - ROWS * s, 1)
            chain_ref[12 * g + 3 * s : 12 * g + 3 * s + 3, :] = moved[:3]
    chain_ref[12 * GROUPS :, :] = jnp.zeros((256 - 12 * GROUPS, 128), f32)
    plain = chain_ref[:CHAIN, :]
    acc = chain_ref[pl.ds(0, 16, stride=16), :]
    for b in range(1, 16):
        acc = acc + chain_ref[pl.ds(b, 16, stride=16), :]
        chain_ref[pl.ds(b, 16, stride=16), :] = acc
    outer_ref[:8, :] = jnp.zeros((8, 128), f32)
    top = jnp.zeros((1, 128), f32)
    for a in range(CHAIN // 16):
        outer_ref[16 * a + 9 : 16 * a + 25, :] = chain_ref[16 * a : 16 * a + 16, :] + top
        top = top + acc[a : a + 1]
    outer_ref[8:9, :] = jnp.zeros((1, 128), f32)
    edge_ref[:8, :] = jnp.zeros((8, 128), f32)
    edge_ref[9 : 9 + CHAIN, :] = plain + outer_ref[8 : 8 + CHAIN, :]
    edge_ref[8:9, :] = jnp.zeros((1, 128), f32)
    mine = outer_ref[7:23, :]
    edge = edge_ref[7:23, :]
    for g in range(1, GROUPS):
        here = group == g
        mine = jnp.where(here, outer_ref[12 * g + 7 : 12 * g + 23, :], mine)
        edge = jnp.where(here, edge_ref[12 * g + 7 : 12 * g + 23, :], edge)
    lane = lax.broadcasted_iota(jnp.int32, (1, 128), 1) // ROWS

    def spread(rows, b):
        out = rows[1 + b : 2 + b]
        for s in range(1, 4):
            out = jnp.where(lane == s, pltpu.roll(rows[1 + 3 * s + b : 2 + 3 * s + b], ROWS * s, 1), out)
        return out

    befores = [spread(mine, b) for b in range(3)] + [mine[13:14], mine[14:15]]
    edges = [spread(edge, b) for b in range(3)] + [edge[13:14], edge[14:15]]
    for b in range(5):
        part_ref[16 * b + 1 : 16 * b + 17, :] = sum_ref[16 * b : 16 * b + 16, :] + befores[b]
        part_ref[16 * b : 16 * b + 1, :] = edges[b]
    quarter = SPAN // 4
    rows = (quarter + PIECE) // 16
    base = part_ref[:rows, :]
    for d in range(16):
        run_ref[pl.ds(d, rows, stride=16), :] = run_ref[pl.ds(d, rows, stride=16), :] + base
    ahead = pltpu.roll(all_ref[jnp.maximum(group - 1, 0)], ROWS, 1)
    last = jnp.where(group > 0, ahead[3:4] + (ahead[4:5] + mine[0:1]), 0.0)
    stretch = quarter + PIECE
    run_ref[stretch : stretch + 128, :] = jnp.concatenate([jnp.zeros((127, 128), f32), last], axis=0)
    main = jnp.concatenate(
        [jnp.transpose(run_ref[128 * i : 128 * i + 128, :]) for i in range(quarter // 128)], axis=1
    )
    tail = [jnp.transpose(run_ref[quarter + 128 * i : quarter + 128 * i + 128, :])[:ROWS] for i in range(4)]
    running = jnp.concatenate([main[ROWS * s : ROWS * s + ROWS] for s in range(4)] + tail, axis=1)
    energy = pltpu.roll(running, NH - (L - 1), 1) - pltpu.roll(running, 1, 1)
    return jnp.maximum(energy, 0.0)[:, :NZ] / L


def stacked(inverse, weight, sel, corr_ref, n_ref, z_ref):
    pairs = SETS * KINDS * OCT
    for j in range(SETS):
        for k in range(KINDS):
            row = 32 * j + 8 * k
            corr_ref[row : row + 8, :] = corr_ref[row : row + 8, :] * inverse[OCT * j : OCT * j + OCT] * weight[row : row + 8]
        normed = corr_ref[32 * j : 32 * j + 32, :]
        head = normed.astype(bf16)
        n_ref[32 * j : 32 * j + 32, :] = head
        n_ref[pairs + 32 * j : pairs + 32 * j + 32, :] = (normed - head.astype(f32)).astype(bf16)
    for n in range(NZ // 256):
        z_ref[0, : 4 * LEVELS, 256 * n : 256 * n + 256] = jnp.dot(
            sel, n_ref[:, 256 * n : 256 * n + 256], preferred_element_type=f32
        )
    total = z_ref[0, :8, :]
    for i in range(1, LEVELS // 2):
        total = total + pltpu.roll(z_ref[0, 8 * i : 8 * i + 8, :], NZ - 2 * i, 1)
    return total + pltpu.roll(pltpu.roll(total, NZ - 1, 1), 4, 0)


def kernel(
    rec_ref, tmpl_ref, shift_ref, valid_ref, out_ref,
    xbuf, wbuf, msg, all_ref, part, land, half, full,
    h_ref, a_ref, z_ref, n_ref, corr_ref, run_ref, sum_ref, chain_ref, outer_ref, edge_ref, part_ref,
    w_send, w_recv, f_send, f_recv, x_send, x_recv, h_send, s_send, s_recv, g_send, g_recv,
    p_send, p_recv, q_send, q_recv, own,
):
    m, q = lax.axis_index("tm"), lax.axis_index("tmpl")
    group, r = m // RING, m % RING
    outer, inner = group // 4, group % 4
    dest_r, dest_q = (m // SETS) % RING, m // ROWS
    lies_here = (r == dest_r) & (q == dest_q) & (inner == m % SETS)
    head = (r == 0) & (group > 0)
    barrier = pltpu.get_barrier_semaphore()

    def signal(tm, tmpl):
        pl.semaphore_signal(barrier, inc=1, device_id=(tm, tmpl), device_id_type=pl.DeviceIdType.MESH)

    def remote(src, dst, send, recv, tm, tmpl):
        return pltpu.make_async_remote_copy(
            src_ref=src, dst_ref=dst, send_sem=send, recv_sem=recv,
            device_id=(tm, tmpl), device_id_type=pl.DeviceIdType.MESH,
        )

    def each(count, skip, step):
        for i in range(count):
            pl.when(i != skip)(functools.partial(step, i))

    source = ROWS * q + SETS * r + inner
    for k in range(KINDS):
        pl.when(jnp.logical_not((source == m) & (q == k)))(functools.partial(signal, source, k))
    each(4, outer, lambda i: signal((4 * i + inner) * RING + r, q))
    each(4, inner, lambda i: signal((4 * outer + i) * RING + r, q))
    each(RING, r, lambda i: signal(group * RING + i, q))
    each(KINDS, q, lambda i: signal(m, i))

    @pl.when(group < GROUPS - 1)
    def _():
        signal((group + 1) * RING, q)

    local = pltpu.make_async_copy(rec_ref.at[pl.ds(ROWS * (q * RING + r), ROWS), :], xbuf.at[r], own)
    local.start()

    waves = tmpl_ref[0].astype(f32)
    eye = lax.broadcasted_iota(jnp.int32, (OCT, OCT), 0) == lax.broadcasted_iota(jnp.int32, (OCT, OCT), 1)
    moves = jnp.sum(jnp.where(eye, shift_ref[...].astype(f32), 0.0), axis=1, keepdims=True)
    masks = jnp.sum(jnp.where(eye, valid_ref[...].astype(f32), 0.0), axis=1, keepdims=True)
    lane = lax.broadcasted_iota(jnp.int32, (OCT, 128), 1)
    extra = jnp.where(lane == 0, moves, jnp.where(lane == 1, masks, 0.0))
    tail = jnp.concatenate([waves[:, 256:], jnp.zeros((OCT, 128 - (L - 256)), f32)], axis=1)
    msg[...] = jnp.concatenate([waves[:, :256], jnp.concatenate([tail, extra], axis=1)], axis=0).astype(bf16)

    @pl.when(group == GROUPS - 1)
    def _():
        xbuf[RING] = jnp.zeros((ROWS, PIECE), bf16)

    count = 4 - lies_here.astype(jnp.int32) + 3 + 3 + (RING - 1) + (KINDS - 1) + RING * head.astype(jnp.int32)
    pl.semaphore_wait(barrier, count)

    def record(i):
        return rec_ref.at[pl.ds(ROWS * (q * RING + i), ROWS), :]

    slot = (m % SETS) * KINDS + q
    mine = pl.ds(inner * KINDS, KINDS)

    def template_copy(i):
        return remote(
            msg, wbuf.at[slot], w_send.at[i], w_recv.at[q], (4 * i + m % SETS) * RING + dest_r, dest_q
        )

    def forward_copy(i):
        return remote(wbuf.at[mine], wbuf.at[mine], f_send.at[i], f_recv.at[inner], (4 * outer + i) * RING + r, q)

    def record_copy(i):
        return remote(record(i), xbuf.at[r], x_send.at[i], x_recv.at[r], group * RING + i, q)

    def halo_copy(i):
        return remote(record(i), xbuf.at[RING], h_send.at[i], x_recv.at[RING], (group - 1) * RING + i, q)

    def near_copy(i):
        return remote(
            all_ref.at[group], all_ref.at[group], s_send.at[i], s_recv.at[inner], (4 * outer + i) * RING + r, q
        )

    def far_copy(i):
        block = all_ref.at[pl.ds(4 * outer, 4)]
        return remote(block, block, g_send.at[i], g_recv.at[outer], (4 * i + inner) * RING + r, q)

    def part_copy(i):
        return remote(part.at[i], land.at[r], p_send.at[i], p_recv.at[r], group * RING + i, q)

    def half_copy(i):
        return remote(half, full.at[q], q_send.at[i], q_recv.at[q], m, i)

    away = [jnp.logical_not((i == outer) & lies_here) for i in range(4)]
    for i in range(4):
        pl.when(away[i])(lambda i=i: template_copy(i).start())

    @pl.when(lies_here)
    def _():
        wbuf[slot] = msg[...]

    each(RING, r, lambda i: record_copy(i).start())

    @pl.when(head)
    def _():
        for i in range(RING):
            halo_copy(i).start()

    for k in range(KINDS):
        here = (source == m) & (q == k)
        pl.when(jnp.logical_not(here))(
            lambda k=k: remote(msg, wbuf.at[inner * KINDS + k], w_send.at[0], w_recv.at[k], m, q).wait_recv()
        )
    each(4, inner, lambda i: forward_copy(i).start())

    local.wait()
    each(RING, r, lambda i: remote(record(0), xbuf.at[i], x_send.at[i], x_recv.at[i], m, q).wait_recv())

    @pl.when(group < GROUPS - 1)
    def _():
        remote(record(0), xbuf.at[RING], h_send.at[0], x_recv.at[RING], m, q).wait_recv()

    x = jnp.concatenate([xbuf[i].astype(f32) for i in range(RING + 1)], axis=1)
    all_ref[group] = block_sums(x, run_ref, sum_ref)
    each(4, inner, lambda i: near_copy(i).start())

    def forwarded(i):
        block = wbuf.at[pl.ds(i * KINDS, KINDS)]
        remote(block, block, f_send.at[i], f_recv.at[i], m, q).wait_recv()

    each(4, inner, forwarded)
    sel, weight = prepare(wbuf[...].astype(f32), a_ref)
    correlate(0, x, h_ref, a_ref, z_ref, corr_ref)

    def near(i):
        block = all_ref.at[4 * outer + i]
        remote(block, block, s_send.at[i], s_recv.at[i], m, q).wait_recv()

    each(4, inner, near)
    each(4, outer, lambda i: far_copy(i).start())
    for j in range(1, SETS):
        correlate(j, x, h_ref, a_ref, z_ref, corr_ref)

    def far(i):
        block = all_ref.at[pl.ds(4 * i, 4)]
        remote(block, block, g_send.at[i], g_recv.at[i], m, q).wait_recv()

    each(4, outer, far)
    energy = window_energy(group, all_ref, run_ref, sum_ref, chain_ref, outer_ref, edge_ref, part_ref)
    total = stacked(1.0 / jnp.sqrt(energy + EPS), weight, sel, corr_ref, n_ref, z_ref)
    for i in range(RING):
        part[i] = total[:, PIECE * i : PIECE * i + PIECE]

    each(RING, r, lambda i: part_copy(i).start())
    land[r] = part[r]
    each(RING, r, lambda i: remote(part.at[0], land.at[i], p_send.at[i], p_recv.at[i], m, q).wait_recv())
    half[...] = jnp.sum(land[...], axis=0)
    each(KINDS, q, lambda i: half_copy(i).start())
    full[q] = half[...]
    each(KINDS, q, lambda i: remote(half, full.at[i], q_send.at[i], q_recv.at[i], m, q).wait_recv())
    whole = jnp.sum(full[...], axis=0)
    row = lax.broadcasted_iota(jnp.int32, (8, PIECE), 0)
    out_ref[...] = jnp.sum(jnp.where(row == q, whole, 0.0), axis=0, keepdims=True)

    for i in range(4):
        pl.when(away[i])(lambda i=i: template_copy(i).wait_send())
    each(4, inner, lambda i: forward_copy(i).wait_send())
    each(RING, r, lambda i: record_copy(i).wait_send())

    @pl.when(head)
    def _():
        for i in range(RING):
            halo_copy(i).wait_send()

    each(4, inner, lambda i: near_copy(i).wait_send())
    each(4, outer, lambda i: far_copy(i).wait_send())
    each(RING, r, lambda i: part_copy(i).wait_send())
    each(KINDS, q, lambda i: half_copy(i).wait_send())


def local(records, templates, shifts, valid):
    vmem = pl.BlockSpec(memory_space=pltpu.VMEM)
    dma = pltpu.SemaphoreType.DMA
    return pl.pallas_call(
        kernel,
        out_shape=jax.ShapeDtypeStruct((1, PIECE), f32),
        in_specs=[pl.BlockSpec(memory_space=pl.ANY), vmem, vmem, vmem],
        out_specs=vmem,
        scratch_shapes=[
            pltpu.VMEM((RING + 1, ROWS, PIECE), bf16),
            pltpu.VMEM((SETS * KINDS, 16, 256), bf16),
            pltpu.VMEM((16, 256), bf16),
            pltpu.VMEM((GROUPS, 8, 128), f32),
            pltpu.VMEM((RING, 8, PIECE), f32),
            pltpu.VMEM((RING, 8, PIECE), f32),
            pltpu.VMEM((8, PIECE), f32),
            pltpu.VMEM((KINDS, 8, PIECE), f32),
            pltpu.VMEM((2, 256, NH), bf16),
            pltpu.VMEM((SETS, 128, BIG), bf16),
            pltpu.VMEM((2, 128, NZ), f32),
            pltpu.VMEM((256, NZ), bf16),
            pltpu.VMEM((128, NZ), f32),
            pltpu.VMEM((1280, 128), f32),
            pltpu.VMEM((128, 128), f32),
            pltpu.VMEM((256, 128), f32),
            pltpu.VMEM((256, 128), f32),
            pltpu.VMEM((256, 128), f32),
            pltpu.VMEM((128, 128), f32),
            dma((4,)), dma((KINDS,)),
            dma((4,)), dma((4,)),
            dma((RING,)), dma((RING + 1,)), dma((RING,)),
            dma((4,)), dma((4,)),
            dma((4,)), dma((4,)),
            dma((RING,)), dma((RING,)),
            dma((KINDS,)), dma((KINDS,)),
            dma,
        ],
        compiler_params=pltpu.CompilerParams(
            collective_id=0, has_side_effects=True, vmem_limit_bytes=40 * 1024 * 1024
        ),
    )(records, templates, shifts, valid)


def solution(mesh):
    in_specs = (P(None, "tm"), P("tmpl", "tm", None), P("tmpl", "tm"), P("tmpl", "tm"))
    return jax.shard_map(local, mesh=mesh, in_specs=in_specs, out_specs=P("tmpl", "tm"), check_vma=False)
```

profile of v0, /device:TPU:1, one launch (start us, length us, event | category | flops | bytes accessed | tf_op | source)
XLA Modules:
  0.0 48.8 jit_solution(5039279037306305401)
XLA Ops:
  0.0 0.0 copy-start
  0.0 1.1 %copy-done = bf16[1024,384]{1,0:T(8,128)(2,1)S(1)} copy-done((bf16[1024,384]{1,0:T(8,128)(2,1)S(1)}, bf16[1024,384]{1,0:T(8,128)(2,1)}, u32[]{:S(2)}) %copy-start) | copy-done | bytes 786456
  1.1 0.0 copy-start.1
  1.1 0.7 %copy-done.1 = bf16[1,8,300]{2,1,0:T(8,128)(2,1)S(1)} copy-done((bf16[1,8,300]{2,1,0:T(8,128)(2,1)S(1)}, bf16[1,8,300]{2,1,0:T(8,128)(2,1)}, u32[]{:S(2)}) %copy-start.1) | copy-done | bytes 4824
  1.8 0.0 copy-start.2
  1.8 0.7 %copy-done.2 = s32[1,8]{1,0:T(1,128)S(1)} copy-done((s32[1,8]{1,0:T(1,128)S(1)}, s32[1,8]{1,0:T(1,128)}, u32[]{:S(2)}) %copy-start.2) | copy-done | bytes 56
  2.5 0.0 copy-start.3
  2.5 0.7 %copy-done.3 = s32[1,8]{1,0:T(1,128)S(1)} copy-done((s32[1,8]{1,0:T(1,128)S(1)}, s32[1,8]{1,0:T(1,128)}, u32[]{:S(2)}) %copy-start.3) | copy-done | bytes 56
  3.1 45.1 %shard_map.46 = f32[1,384]{1,0:T(1,128)S(1)} custom-call(bf16[1024,384]{1,0:T(8,128)(2,1)S(1)} %copy-done, bf16[1,8,300]{2,1,0:T(8,128)(2,1)S(1)} %copy-done.1, s32[1,8]{1,0:T(1,128)S(1)} %copy-done.2, s32[1,8]{1,0:T(1,128)S(1)} %copy-done.3), custom_call_target="tpu_custom_call" | custom-call | tf_op jit(solution)/shard_map/pallas_call | solution.py:375
  48.2 0.6 %copy.6 = f32[1,384]{1,0:T(1,128)} copy(f32[1,384]{1,0:T(1,128)S(1)} %shard_map.46) | data formatting | bytes 3072
Async XLA Ops:
  0.0 1.1 %copy-start = (bf16[1024,384]{1,0:T(8,128)(2,1)S(1)}, bf16[1024,384]{1,0:T(8,128)(2,1)}, u32[]{:S(2)}) copy-start(bf16[1024,384]{1,0:T(8,128)(2,1)} %rec_ref.1) | copy-start | bytes 2359300
  1.1 0.7 %copy-start.1 = (bf16[1,8,300]{2,1,0:T(8,128)(2,1)S(1)}, bf16[1,8,300]{2,1,0:T(8,128)(2,1)}, u32[]{:S(2)}) copy-start(bf16[1,8,300]{2,1,0:T(8,128)(2,1)} %tmpl_ref.1) | copy-start | bytes 14404
  1.8 0.7 %copy-start.2 = (s32[1,8]{1,0:T(1,128)S(1)}, s32[1,8]{1,0:T(1,128)}, u32[]{:S(2)}) copy-start(s32[1,8]{1,0:T(1,128)} %shift_ref.1) | copy-start | bytes 100
  2.5 0.7 %copy-start.3 = (s32[1,8]{1,0:T(1,128)S(1)}, s32[1,8]{1,0:T(1,128)}, u32[]{:S(2)}) copy-start(s32[1,8]{1,0:T(1,128)} %valid_ref.1) | copy-start | bytes 100
where the time goes:
time: 49 us; the launch traced here: 48.8 us
  Pallas kernels  45.1 us (92%)
  local copies, waits for them, and re-layouts  3.7 us (8%)
    pallas_call x1, Pallas kernels, local(): pl.pallas_call(kernel, out_shape=jax.ShapeDtypeStruct((1, PIECE), f32), i...  45.1 us
    unnamed x9, local copies, waits for them, and re-layouts  3.7 us

commit v1 on v0

v1 whole, which is shorter than its diff:
```python
import functools

import jax
import jax.numpy as jnp
from jax import lax
from jax.experimental import pallas as pl
from jax.experimental.pallas import tpu as pltpu
from jax.sharding import PartitionSpec as P

L = 300
MAXS = 20
EPS = 1e-05
KINDS = 4
RING = 8
GROUPS = 16
COLUMN = 8
PIECE = 384
ROWS = 32
OCT = 8
SETS = ROWS // OCT
STEP = 32
SPAN = RING * PIECE
WIDE = SPAN + PIECE
NH = 3584
NZ = 3328
BIG = 3 * 256
QUARTER = SPAN // 4
LEVELS = 22
BLOCKS = (WIDE // 16)
CHAIN = 208

f32 = jnp.float32
bf16 = jnp.bfloat16


def prepare(message, a_ref):
    pairs = SETS * KINDS * OCT
    low = message[:, :OCT, :].reshape(pairs, 256)
    high = message[:, OCT:, :].reshape(pairs, 256)

    parts = [low[:, :128].astype(bf16), low[:, 128:].astype(bf16), high[:, :128].astype(bf16)]
    lane = lax.broadcasted_iota(jnp.int32, (128, 256), 1)
    line = lax.broadcasted_iota(jnp.int32, (128, 256), 0)
    same = (lane % OCT) == (line % OCT)
    for u_lo in range(4):
        spread = jnp.where(line == STEP * u_lo + lane // OCT, 1.0, 0.0).astype(bf16)
        for u_hi in range(3):
            wide = jnp.dot(parts[u_hi], spread, preferred_element_type=f32)
            block = jnp.where(same, wide, 0.0).astype(bf16)
            for j in range(SETS):
                a_ref[j, 32 * u_lo : 32 * u_lo + 32, 256 * u_hi : 256 * u_hi + 256] = block[32 * j : 32 * j + 32]

    shift = high[:, 128:129]
    valid = high[:, 129:130]
    column = lax.broadcasted_iota(jnp.int32, (pairs, 128), 1)
    squares = low[:, :128] ** 2 + low[:, 128:] ** 2 + high[:, :128] ** 2
    power = jnp.sum(squares, axis=1, keepdims=True) / L
    weight = valid / (L * jnp.sqrt(power + EPS))

    kind = (lax.broadcasted_iota(jnp.int32, (pairs, 128), 0) // OCT) % KINDS
    picked = (shift == (column // KINDS).astype(f32)) & (kind == column % KINDS)
    sel = jnp.transpose(jnp.where(picked, 1.0, 0.0)).astype(bf16)
    return jnp.concatenate([sel, sel], axis=1)[: 4 * LEVELS], weight


def shifted(j, x, h_ref):
    x8 = jnp.concatenate([x[OCT * j : OCT * j + OCT], jnp.zeros((OCT, NH - WIDE), f32)], axis=1)
    for i in range(STEP // 2):
        first = x8 if i == 0 else pltpu.roll(x8, NH - 2 * i, 1)
        second = pltpu.roll(x8, NH - 2 * i - 1, 1)
        h_ref[j, 16 * i : 16 * i + 16, :] = jnp.concatenate([first, second], axis=0).astype(bf16)


def correlate(j, h_ref, a_ref, z_ref, corr_ref):
    slot = j % 2
    for n in range(NZ // 256):
        acc = None
        for u_hi in range(3):
            part = jnp.dot(
                a_ref[j, :, 256 * u_hi : 256 * u_hi + 256],
                h_ref[j, :, 256 * n + 128 * u_hi : 256 * n + 128 * u_hi + 256],
                preferred_element_type=f32,
            )
            acc = part if acc is None else acc + part
        z_ref[slot, :, 256 * n : 256 * n + 256] = acc
    for k in range(KINDS):
        corr = z_ref[slot, 8 * k : 8 * k + 8, :]
        for u_lo in range(1, 4):
            corr = corr + pltpu.roll(z_ref[slot, 32 * u_lo + 8 * k : 32 * u_lo + 8 * k + 8, :], NZ - STEP * u_lo, 1)
        corr_ref[32 * j + 8 * k : 32 * j + 8 * k + 8, :] = corr


def running16(run_ref, start, rows, sum_ref):
    acc = run_ref[pl.ds(start, rows, stride=16), :]
    for d in range(1, 16):
        acc = acc + run_ref[pl.ds(start + d, rows, stride=16), :]
        run_ref[pl.ds(start + d, rows, stride=16), :] = acc
    sum_ref[:rows, :] = acc
    sum_ref[rows:, :] = jnp.zeros((128 - rows, 128), f32)
    outer = sum_ref[pl.ds(0, 8, stride=16), :]
    for c in range(1, 16):
        outer = outer + sum_ref[pl.ds(c, 8, stride=16), :]
        sum_ref[pl.ds(c, 8, stride=16), :] = outer
    return acc, outer


def block_sums(x, run_ref, sum_ref):
    squares = x * x
    stacked = jnp.concatenate([squares[:, QUARTER * s : QUARTER * s + QUARTER] for s in range(4)], axis=0)
    for i in range(QUARTER // 128):
        run_ref[128 * i : 128 * i + 128, :] = jnp.transpose(stacked[:, 128 * i : 128 * i + 128])
    acc, outer = running16(run_ref, 0, QUARTER // 16, sum_ref)
    final = acc[QUARTER // 16 - 1 : QUARTER // 16]
    before = sum_ref[QUARTER // 16 - 2 : QUARTER // 16 - 1, :]
    return jnp.concatenate([outer[:3], final, before, jnp.zeros((3, 128), f32)], axis=0)


def halo_sums(x, run_ref, tail_ref):
    halo = jnp.concatenate([x * x, jnp.zeros((128 - ROWS, PIECE), f32)], axis=0)
    for i in range(PIECE // 128):
        run_ref[QUARTER + 128 * i : QUARTER + 128 * i + 128, :] = jnp.transpose(halo[:, 128 * i : 128 * i + 128])
    running16(run_ref, QUARTER, PIECE // 16, tail_ref)


def window_energy(group, all_ref, run_ref, sum_ref, tail_ref, chain_ref, outer_ref, edge_ref, part_ref):
    for g in range(GROUPS):
        totals = all_ref[g]
        for s in range(4):
            moved = totals if s == 0 else pltpu.roll(totals, 128 - ROWS * s, 1)
            chain_ref[12 * g + 3 * s : 12 * g + 3 * s + 3, :] = moved[:3]
    chain_ref[12 * GROUPS :, :] = jnp.zeros((256 - 12 * GROUPS, 128), f32)
    plain = chain_ref[:CHAIN, :]
    acc = chain_ref[pl.ds(0, 16, stride=16), :]
    for b in range(1, 16):
        acc = acc + chain_ref[pl.ds(b, 16, stride=16), :]
        chain_ref[pl.ds(b, 16, stride=16), :] = acc
    outer_ref[:8, :] = jnp.zeros((8, 128), f32)
    top = jnp.zeros((1, 128), f32)
    for a in range(CHAIN // 16):
        outer_ref[16 * a + 9 : 16 * a + 25, :] = chain_ref[16 * a : 16 * a + 16, :] + top
        top = top + acc[a : a + 1]
    outer_ref[8:9, :] = jnp.zeros((1, 128), f32)
    edge_ref[:8, :] = jnp.zeros((8, 128), f32)
    edge_ref[9 : 9 + CHAIN, :] = plain + outer_ref[8 : 8 + CHAIN, :]
    edge_ref[8:9, :] = jnp.zeros((1, 128), f32)
    mine = outer_ref[7:23, :]
    edge = edge_ref[7:23, :]
    for g in range(1, GROUPS):
        here = group == g
        mine = jnp.where(here, outer_ref[12 * g + 7 : 12 * g + 23, :], mine)
        edge = jnp.where(here, edge_ref[12 * g + 7 : 12 * g + 23, :], edge)
    lane = lax.broadcasted_iota(jnp.int32, (1, 128), 1) // ROWS

    def spread(rows, b):
        out = rows[1 + b : 2 + b]
        for s in range(1, 4):
            out = jnp.where(lane == s, pltpu.roll(rows[1 + 3 * s + b : 2 + 3 * s + b], ROWS * s, 1), out)
        return out

    befores = [spread(mine, b) for b in range(3)] + [mine[13:14], mine[14:15]]
    edges = [spread(edge, b) for b in range(3)] + [edge[13:14], edge[14:15]]
    for b in range(5):
        sums = sum_ref[16 * b : 16 * b + 16, :] if b < 3 else tail_ref[16 * b - 48 : 16 * b - 32, :]
        part_ref[16 * b + 1 : 16 * b + 17, :] = sums + befores[b]
        part_ref[16 * b : 16 * b + 1, :] = edges[b]
    quarter = QUARTER
    rows = (quarter + PIECE) // 16
    base = part_ref[:rows, :]
    for d in range(16):
        run_ref[pl.ds(d, rows, stride=16), :] = run_ref[pl.ds(d, rows, stride=16), :] + base
    ahead = pltpu.roll(all_ref[jnp.maximum(group - 1, 0)], ROWS, 1)
    last = jnp.where(group > 0, ahead[3:4] + (ahead[4:5] + mine[0:1]), 0.0)
    stretch = quarter + PIECE
    run_ref[stretch : stretch + 128, :] = jnp.concatenate([jnp.zeros((127, 128), f32), last], axis=0)
    main = jnp.concatenate(
        [jnp.transpose(run_ref[128 * i : 128 * i + 128, :]) for i in range(quarter // 128)], axis=1
    )
    tail = [jnp.transpose(run_ref[quarter + 128 * i : quarter + 128 * i + 128, :])[:ROWS] for i in range(4)]
    running = jnp.concatenate([main[ROWS * s : ROWS * s + ROWS] for s in range(4)] + tail, axis=1)
    energy = pltpu.roll(running, NH - (L - 1), 1) - pltpu.roll(running, 1, 1)
    return jnp.maximum(energy, 0.0)[:, :NZ] / L


def stacked(inverse, weight, sel, corr_ref, n_ref, z_ref):
    pairs = SETS * KINDS * OCT
    for j in range(SETS):
        for k in range(KINDS):
            row = 32 * j + 8 * k
            corr_ref[row : row + 8, :] = corr_ref[row : row + 8, :] * inverse[OCT * j : OCT * j + OCT] * weight[row : row + 8]
        normed = corr_ref[32 * j : 32 * j + 32, :]
        head = normed.astype(bf16)
        n_ref[32 * j : 32 * j + 32, :] = head
        n_ref[pairs + 32 * j : pairs + 32 * j + 32, :] = (normed - head.astype(f32)).astype(bf16)
    for n in range(NZ // 256):
        z_ref[0, : 4 * LEVELS, 256 * n : 256 * n + 256] = jnp.dot(
            sel, n_ref[:, 256 * n : 256 * n + 256], preferred_element_type=f32
        )
    total = z_ref[0, :8, :]
    for i in range(1, LEVELS // 2):
        total = total + pltpu.roll(z_ref[0, 8 * i : 8 * i + 8, :], NZ - 2 * i, 1)
    return total + pltpu.roll(pltpu.roll(total, NZ - 1, 1), 4, 0)


def kernel(
    rec_ref, tmpl_ref, shift_ref, valid_ref, out_ref,
    xbuf, wbuf, ybuf, msg, all_ref, part, land, half, full, tbuf, ibuf,
    h_ref, a_ref, z_ref, n_ref, corr_ref, run_ref, sum_ref, tail_ref, chain_ref, outer_ref, edge_ref, part_ref,
    w_send, w_recv, f_send, f_recv, x_send, x_recv, h_send, s_send, s_recv, g_send, g_recv,
    p_send, p_recv, q_send, q_recv, own,
):
    m, q = lax.axis_index("tm"), lax.axis_index("tmpl")
    group, r = m // RING, m % RING
    high, y = group // COLUMN, group % COLUMN
    x_at, core = r // 2, r % 2
    p = 2 * q + core
    to_self = p // 4 == high
    barrier = pltpu.get_barrier_semaphore()

    def signal(tm, tmpl):
        pl.semaphore_signal(barrier, inc=1, device_id=(tm, tmpl), device_id_type=pl.DeviceIdType.MESH)

    def remote(src, dst, send, recv, tm, tmpl):
        return pltpu.make_async_remote_copy(
            src_ref=src, dst_ref=dst, send_sem=send, recv_sem=recv,
            device_id=(tm, tmpl), device_id_type=pl.DeviceIdType.MESH,
        )

    def each(count, skip, step):
        for i in range(count):
            pl.when(i != skip)(functools.partial(step, i))

    def at_y(i):
        return (high * COLUMN + i) * RING + r

    local = [
        pltpu.make_async_copy(tmpl_ref, tbuf, own.at[0]),
        pltpu.make_async_copy(shift_ref, ibuf.at[0], own.at[1]),
        pltpu.make_async_copy(valid_ref, ibuf.at[1], own.at[2]),
        pltpu.make_async_copy(rec_ref.at[pl.ds(2 * p, 2), x_at], xbuf.at[r], own.at[3]),
    ]
    for copy in local:
        copy.start()

    other = (1 - high) * COLUMN * RING + y * RING + r
    signal(other, q)
    each(COLUMN, y, lambda i: signal(at_y(i), q))
    comes = [
        [jnp.logical_not(to_self & (core == cs) & (q == k)) for k in range(KINDS)] for cs in range(2)
    ]
    for cs in range(2):
        for k in range(KINDS):
            source = ((p // 4) * COLUMN + y) * RING + 2 * x_at + cs
            pl.when(comes[cs][k])(functools.partial(signal, source, k))
    each(RING, r, lambda i: signal(group * RING + i, q))
    each(KINDS, q, lambda i: signal(m, i))

    @pl.when(group < GROUPS - 1)
    def _():
        signal(m + RING, q)

    for copy in local:
        copy.wait()

    waves = tbuf[0].astype(f32)
    eye = lax.broadcasted_iota(jnp.int32, (OCT, OCT), 0) == lax.broadcasted_iota(jnp.int32, (OCT, OCT), 1)
    moves = jnp.sum(jnp.where(eye, ibuf[0].astype(f32), 0.0), axis=1, keepdims=True)
    masks = jnp.sum(jnp.where(eye, ibuf[1].astype(f32), 0.0), axis=1, keepdims=True)
    lane = lax.broadcasted_iota(jnp.int32, (OCT, 128), 1)
    extra = jnp.where(lane == 0, moves, jnp.where(lane == 1, masks, 0.0))
    tail = jnp.concatenate([waves[:, 256:], jnp.zeros((OCT, 128 - (L - 256)), f32)], axis=1)
    msg[...] = jnp.concatenate([waves[:, :256], jnp.concatenate([tail, extra], axis=1)], axis=0).astype(bf16)

    @pl.when(group == GROUPS - 1)
    def _():
        xbuf[RING] = jnp.zeros((2, ROWS // 2, PIECE), bf16)

    count = (
        1 + (COLUMN - 1) + 8 - to_self.astype(jnp.int32)
        + (RING - 1) + (KINDS - 1) + (group > 0).astype(jnp.int32)
    )
    pl.semaphore_wait(barrier, count)

    def record(i):
        return rec_ref.at[pl.ds(2 * (2 * q + i % 2), 2), i // 2]

    def template_copy(i):
        return remote(msg, ybuf.at[y], w_send.at[i], w_recv.at[y], at_y(i), q)

    def pair_copy(i, z):
        tm = (z * COLUMN + y) * RING + 2 * x_at + i % 2
        return remote(
            ybuf.at[pl.ds(2 * i, 2)], wbuf.at[KINDS * core + q], f_send.at[2 * i + z], f_recv.at[KINDS * core + q],
            tm, 2 * high + i // 2,
        )

    def record_copy(i):
        return remote(record(i), xbuf.at[r], x_send.at[i], x_recv.at[r], group * RING + i, q)

    def halo_copy():
        return remote(xbuf.at[0], xbuf.at[RING], h_send, x_recv.at[RING], m - RING, q)

    def near_copy(i):
        return remote(all_ref.at[group], all_ref.at[group], s_send.at[i], s_recv.at[y], at_y(i), q)

    def far_copy():
        block = all_ref.at[pl.ds(COLUMN * high, COLUMN)]
        return remote(block, block, g_send, g_recv, other, q)

    def part_copy(i):
        return remote(
            part.at[i, pl.ds(0, KINDS)], land.at[r, pl.ds(0, KINDS)], p_send.at[i], p_recv.at[r], group * RING + i, q
        )

    def half_copy(i):
        return remote(half, full.at[q], q_send.at[i], q_recv.at[q], m, i)

    goes = [[jnp.logical_not(to_self & (p % 4 == i) & (high == z)) for z in range(2)] for i in range(4)]

    each(RING, r, lambda i: record_copy(i).start())
    each(COLUMN, y, lambda i: template_copy(i).start())
    ybuf[y] = msg[...]
    each(RING, r, lambda i: remote(xbuf.at[i], xbuf.at[i], x_send.at[i], x_recv.at[i], m, q).wait_recv())

    @pl.when(group > 0)
    def _():
        halo_copy().start()

    main = jnp.concatenate([xbuf[i].astype(f32).reshape(ROWS, PIECE) for i in range(RING)], axis=1)
    all_ref[group] = block_sums(main, run_ref, sum_ref)
    each(COLUMN, y, lambda i: near_copy(i).start())

    each(COLUMN, y, lambda i: remote(msg, ybuf.at[i], w_send.at[i], w_recv.at[i], m, q).wait_recv())
    for i in range(4):
        for z in range(2):
            pl.when(goes[i][z])(lambda i=i, z=z: pair_copy(i, z).start())

    @pl.when(to_self)
    def _():
        wbuf[KINDS * core + q] = ybuf[pl.ds(2 * (p % 4), 2)]

    @pl.when(group < GROUPS - 1)
    def _():
        remote(xbuf.at[0], xbuf.at[RING], h_send, x_recv.at[RING], m, q).wait_recv()

    halo = xbuf[RING].astype(f32).reshape(ROWS, PIECE)
    halo_sums(halo, run_ref, tail_ref)
    x = jnp.concatenate([main, halo], axis=1)
    for j in range(SETS):
        shifted(j, x, h_ref)

    def near(i):
        block = all_ref.at[high * COLUMN + i]
        remote(block, block, s_send.at[i], s_recv.at[i], m, q).wait_recv()

    each(COLUMN, y, near)
    far_copy().start()

    for cs in range(2):
        for k in range(KINDS):
            slot = KINDS * cs + k
            pl.when(comes[cs][k])(
                lambda slot=slot: remote(
                    wbuf.at[slot], wbuf.at[slot], f_send.at[0], f_recv.at[slot], m, q
                ).wait_recv()
            )
    shards = wbuf[...].astype(f32)
    shards = [shards[KINDS * cs + k, e : e + 1] for e in range(2) for cs in range(2) for k in range(KINDS)]
    sel, weight = prepare(jnp.concatenate(shards, axis=0), a_ref)
    for j in range(SETS):
        correlate(j, h_ref, a_ref, z_ref, corr_ref)

    far = all_ref.at[pl.ds(COLUMN * (1 - high), COLUMN)]
    remote(far, far, g_send, g_recv, m, q).wait_recv()
    energy = window_energy(group, all_ref, run_ref, sum_ref, tail_ref, chain_ref, outer_ref, edge_ref, part_ref)
    total = stacked(1.0 / jnp.sqrt(energy + EPS), weight, sel, corr_ref, n_ref, z_ref)
    for i in range(RING):
        part[i] = total[:, PIECE * i : PIECE * i + PIECE]

    each(RING, r, lambda i: part_copy(i).start())
    land[r, :KINDS] = part[r, :KINDS]
    each(
        RING, r,
        lambda i: remote(
            part.at[0, pl.ds(0, KINDS)], land.at[i, pl.ds(0, KINDS)], p_send.at[i], p_recv.at[i], m, q
        ).wait_recv(),
    )
    half[...] = jnp.concatenate([jnp.sum(land[:, :KINDS], axis=0), jnp.zeros((KINDS, PIECE), f32)], axis=0)
    each(KINDS, q, lambda i: half_copy(i).start())
    full[q] = half[...]
    each(KINDS, q, lambda i: remote(half, full.at[i], q_send.at[i], q_recv.at[i], m, q).wait_recv())
    whole = jnp.sum(full[...], axis=0)
    row = lax.broadcasted_iota(jnp.int32, (8, PIECE), 0)
    out_ref[...] = jnp.sum(jnp.where(row == q, whole, 0.0), axis=0, keepdims=True)

    each(COLUMN, y, lambda i: template_copy(i).wait_send())
    each(RING, r, lambda i: record_copy(i).wait_send())

    @pl.when(group > 0)
    def _():
        halo_copy().wait_send()

    for i in range(4):
        for z in range(2):
            pl.when(goes[i][z])(lambda i=i, z=z: pair_copy(i, z).wait_send())
    each(COLUMN, y, lambda i: near_copy(i).wait_send())
    far_copy().wait_send()
    each(RING, r, lambda i: part_copy(i).wait_send())
    each(KINDS, q, lambda i: half_copy(i).wait_send())


def local(records, templates, shifts, valid):
    hbm = pl.BlockSpec(memory_space=pltpu.HBM)
    dma = pltpu.SemaphoreType.DMA
    return pl.pallas_call(
        kernel,
        out_shape=jax.ShapeDtypeStruct((1, PIECE), f32),
        in_specs=[hbm] * 4,
        out_specs=pl.BlockSpec(memory_space=pltpu.VMEM),
        scratch_shapes=[
            pltpu.VMEM((RING + 1, 2, ROWS // 2, PIECE), bf16),
            pltpu.VMEM((2 * KINDS, 2, 16, 256), bf16),
            pltpu.VMEM((COLUMN, 16, 256), bf16),
            pltpu.VMEM((16, 256), bf16),
            pltpu.VMEM((GROUPS, 8, 128), f32),
            pltpu.VMEM((RING, 8, PIECE), f32),
            pltpu.VMEM((RING, 8, PIECE), f32),
            pltpu.VMEM((8, PIECE), f32),
            pltpu.VMEM((KINDS, 8, PIECE), f32),
            pltpu.VMEM((1, OCT, L), bf16),
            pltpu.VMEM((2, 1, OCT), jnp.int32),
            pltpu.VMEM((SETS, 256, NH), bf16),
            pltpu.VMEM((SETS, 128, BIG), bf16),
            pltpu.VMEM((2, 128, NZ), f32),
            pltpu.VMEM((256, NZ), bf16),
            pltpu.VMEM((128, NZ), f32),
            pltpu.VMEM((1280, 128), f32),
            pltpu.VMEM((128, 128), f32),
            pltpu.VMEM((128, 128), f32),
            pltpu.VMEM((256, 128), f32),
            pltpu.VMEM((256, 128), f32),
            pltpu.VMEM((256, 128), f32),
            pltpu.VMEM((128, 128), f32),
            dma((COLUMN,)), dma((COLUMN,)),
            dma((8,)), dma((2 * KINDS,)),
            dma((RING,)), dma((RING + 1,)), dma,
            dma((COLUMN,)), dma((COLUMN,)),
            dma, dma,
            dma((RING,)), dma((RING,)),
            dma((KINDS,)), dma((KINDS,)),
            dma((4,)),
        ],
        compiler_params=pltpu.CompilerParams(
            collective_id=0, has_side_effects=True, vmem_limit_bytes=63 * 1024 * 1024
        ),
    )(records.reshape(GROUPS, 4, 16, PIECE), templates, shifts, valid)


def solution(mesh):
    in_specs = (P(None, "tm"), P("tmpl", "tm", None), P("tmpl", "tm"), P("tmpl", "tm"))
    return jax.shard_map(local, mesh=mesh, in_specs=in_specs, out_specs=P("tmpl", "tm"), check_vma=False)
```

time: 49 us -> 41.1 us (0.84)
  Pallas kernels: 45.1 us -> 39.7 us
  local copies, waits for them, and re-layouts: 3.7 us -> 1.24 us
    pallas_call x1, Pallas kernels: 45.1 us -> 39.7 us  [local(): pl.pallas_call(kernel, out_shape=jax.ShapeDtypeStruct((1, PIECE), f32), i...]
    unnamed x9 -> x1, local copies, waits for them, and re-layouts: 3.7 us -> 1.24 us
where the time goes in v1:
time: 41.1 us; the launch traced here: 40.9 us
  Pallas kernels  39.7 us (97%)
  local copies, waits for them, and re-layouts  1.24 us (3%)
    pallas_call x1, Pallas kernels, local(): pl.pallas_call(kernel, out_shape=jax.ShapeDtypeStruct((1, PIECE), f32), i...  39.7 us
    unnamed x1, local copies, waits for them, and re-layouts  1.24 us

profile of v1, /device:TPU:1, one launch (start us, length us, event | category | flops | bytes accessed | tf_op | source)
XLA Modules:
  0.0 40.9 jit_solution(4578669362105435215)
XLA Ops:
  0.0 39.7 %shard_map.46 = f32[1,384]{1,0:T(1,128)} custom-call(bf16[16,4,16,384]{3,2,1,0:T(8,128)(2,1)} %bitcast.1, bf16[1,8,300]{2,1,0:T(8,128)(2,1)} %tmpl_ref.1, s32[1,8]{1,0:T(1,128)} %shift_ref.1, s32[1,8]{1,0:T(1,128)} %valid_ref.1), custom_call_target="tpu_custom_call" | custom-call | tf_op jit(solution)/shard_map/pallas_call | solution.py:414
  39.7 1.2 %copy.6 = f32[1,384]{1,0:T(1,128)} copy(f32[1,384]{1,0:T(1,128)} %shard_map.46) | data formatting | bytes 3072

commit v2 on v1

--- a/solution.py
+++ b/solution.py
@@ -76,12 +76,13 @@
     for n in range(NZ // 256):
         acc = None
         for u_hi in range(3):
+            rows = 64 if u_hi == 2 else 128
             part = jnp.dot(
-                a_ref[j, :, 256 * u_hi : 256 * u_hi + 256],
+                a_ref[j, :rows, 256 * u_hi : 256 * u_hi + 256],
                 h_ref[j, :, 256 * n + 128 * u_hi : 256 * n + 128 * u_hi + 256],
                 preferred_element_type=f32,
             )
-            acc = part if acc is None else acc + part
+            acc = part if acc is None else jnp.concatenate([acc[:rows] + part, acc[rows:]], axis=0) if rows < 128 else acc + part
         z_ref[slot, :, 256 * n : 256 * n + 256] = acc
     for k in range(KINDS):
         corr = z_ref[slot, 8 * k : 8 * k + 8, :]
@@ -119,7 +120,8 @@
     halo = jnp.concatenate([x * x, jnp.zeros((128 - ROWS, PIECE), f32)], axis=0)
     for i in range(PIECE // 128):
         run_ref[QUARTER + 128 * i : QUARTER + 128 * i + 128, :] = jnp.transpose(halo[:, 128 * i : 128 * i + 128])
-    running16(run_ref, QUARTER, PIECE // 16, tail_ref)
+    _, outer = running16(run_ref, QUARTER, PIECE // 16, tail_ref)
+    return outer[:1]
 
 
 def window_energy(group, all_ref, run_ref, sum_ref, tail_ref, chain_ref, outer_ref, edge_ref, part_ref):
@@ -203,10 +205,10 @@
 
 def kernel(
     rec_ref, tmpl_ref, shift_ref, valid_ref, out_ref,
-    xbuf, wbuf, ybuf, msg, all_ref, part, land, half, full, tbuf, ibuf,
-    h_ref, a_ref, z_ref, n_ref, corr_ref, run_ref, sum_ref, tail_ref, chain_ref, outer_ref, edge_ref, part_ref,
+    xbuf, wbuf, ybuf, msg, all_ref, part, land, tbuf, ibuf,
+    h_ref, a_ref, z_ref, n_ref, corr_ref, run_ref, sum_ref, tail_ref, chain_ref, outer_ref, edge_ref, part_ref, root_ref,
     w_send, w_recv, f_send, f_recv, x_send, x_recv, h_send, s_send, s_recv, g_send, g_recv,
-    p_send, p_recv, q_send, q_recv, own,
+    p_send, p_recv, own, ready,
 ):
     m, q = lax.axis_index("tm"), lax.axis_index("tmpl")
     group, r = m // RING, m % RING
@@ -241,8 +243,18 @@
     for copy in local:
         copy.start()
 
+    low = high == 0
     other = (1 - high) * COLUMN * RING + y * RING + r
-    signal(other, q)
+
+    def pair_target(i, z):
+        return (z * COLUMN + y) * RING + 2 * x_at + i % 2, 2 * high + i // 2
+
+    @pl.when(low)
+    def _():
+        signal(other, q)
+        for i in range(4):
+            signal(*pair_target(i, 1))
+
     each(COLUMN, y, lambda i: signal(at_y(i), q))
     comes = [
         [jnp.logical_not(to_self & (core == cs) & (q == k)) for k in range(KINDS)] for cs in range(2)
@@ -250,15 +262,75 @@
     for cs in range(2):
         for k in range(KINDS):
             source = ((p // 4) * COLUMN + y) * RING + 2 * x_at + cs
-            pl.when(comes[cs][k])(functools.partial(signal, source, k))
-    each(RING, r, lambda i: signal(group * RING + i, q))
-    each(KINDS, q, lambda i: signal(m, i))
+            pl.when(comes[cs][k] & (low | to_self))(functools.partial(signal, source, k))
+    each(RING * KINDS, KINDS * r + q, lambda i: signal(group * RING + i // KINDS, i % KINDS))
 
     @pl.when(group < GROUPS - 1)
     def _():
         signal(m + RING, q)
 
-    for copy in local:
+    @pl.when(group == GROUPS - 1)
+    def _():
+        xbuf[RING] = jnp.zeros((2, ROWS // 2, PIECE), bf16)
+
+    count = (
+        (COLUMN - 1) + 4 - to_self.astype(jnp.int32)
+        + (RING * KINDS - 1) + (group > 0).astype(jnp.int32)
+        + high * (5 + 8 * (1 - to_self.astype(jnp.int32)))
+    )
+
+    @pl.when(low)
+    def _():
+        all_ref[COLUMN:] = jnp.zeros((COLUMN, 8, 128), f32)
+
+    pl.semaphore_wait(barrier, count)
+
+    def answer(tm, tmpl):
+        pl.semaphore_signal(ready, inc=1, device_id=(tm, tmpl), device_id_type=pl.DeviceIdType.MESH)
+
+    @pl.when(high == 1)
+    def _():
+        answer(other, q)
+
+    @pl.when((high == 1) & jnp.logical_not(to_self))
+    def _():
+        for cs in range(2):
+            for k in range(KINDS):
+                answer(y * RING + 2 * x_at + cs, k)
+
+    def record(i):
+        return rec_ref.at[pl.ds(2 * (2 * q + i % 2), 2), i // 2]
+
+    def template_copy(i):
+        return remote(msg, ybuf.at[y], w_send.at[i], w_recv.at[y], at_y(i), q)
+
+    def pair_copy(i, z):
+        return remote(
+            ybuf.at[pl.ds(2 * i, 2)], wbuf.at[KINDS * core + q], f_send.at[2 * i + z], f_recv.at[KINDS * core + q],
+            *pair_target(i, z),
+        )
+
+    def record_copy(i):
+        return remote(record(i), xbuf.at[r], x_send.at[i], x_recv.at[r], group * RING + i, q)
+
+    def halo_copy():
+        return remote(xbuf.at[0], xbuf.at[RING], h_send, x_recv.at[RING], m - RING, q)
+
+    def near_copy(i):
+        return remote(all_ref.at[group], all_ref.at[group], s_send.at[i], s_recv.at[y], at_y(i), q)
+
+    def far_copy():
+        block = all_ref.at[pl.ds(COLUMN * high, COLUMN)]
+        return remote(block, block, g_send, g_recv, other, q)
+
+    def part_copy(i):
+        me = KINDS * r + q
+        return remote(part.at[i], land.at[me], p_send.at[i], p_recv.at[me], group * RING + i // KINDS, i % KINDS)
+
+    goes = [[jnp.logical_not(to_self & (p % 4 == i) & (high == z)) for z in range(2)] for i in range(4)]
+
+    each(RING, r, lambda i: record_copy(i).start())
+    for copy in local[:3]:
         copy.wait()
 
     waves = tbuf[0].astype(f32)
@@ -270,55 +342,9 @@
     tail = jnp.concatenate([waves[:, 256:], jnp.zeros((OCT, 128 - (L - 256)), f32)], axis=1)
     msg[...] = jnp.concatenate([waves[:, :256], jnp.concatenate([tail, extra], axis=1)], axis=0).astype(bf16)
 
-    @pl.when(group == GROUPS - 1)
-    def _():
-        xbuf[RING] = jnp.zeros((2, ROWS // 2, PIECE), bf16)
-
-    count = (
-        1 + (COLUMN - 1) + 8 - to_self.astype(jnp.int32)
-        + (RING - 1) + (KINDS - 1) + (group > 0).astype(jnp.int32)
-    )
-    pl.semaphore_wait(barrier, count)
-
-    def record(i):
-        return rec_ref.at[pl.ds(2 * (2 * q + i % 2), 2), i // 2]
-
-    def template_copy(i):
-        return remote(msg, ybuf.at[y], w_send.at[i], w_recv.at[y], at_y(i), q)
-
-    def pair_copy(i, z):
-        tm = (z * COLUMN + y) * RING + 2 * x_at + i % 2
-        return remote(
-            ybuf.at[pl.ds(2 * i, 2)], wbuf.at[KINDS * core + q], f_send.at[2 * i + z], f_recv.at[KINDS * core + q],
-            tm, 2 * high + i // 2,
-        )
-
-    def record_copy(i):
-        return remote(record(i), xbuf.at[r], x_send.at[i], x_recv.at[r], group * RING + i, q)
-
-    def halo_copy():
-        return remote(xbuf.at[0], xbuf.at[RING], h_send, x_recv.at[RING], m - RING, q)
-
-    def near_copy(i):
-        return remote(all_ref.at[group], all_ref.at[group], s_send.at[i], s_recv.at[y], at_y(i), q)
-
-    def far_copy():
-        block = all_ref.at[pl.ds(COLUMN * high, COLUMN)]
-        return remote(block, block, g_send, g_recv, other, q)
-
-    def part_copy(i):
-        return remote(
-            part.at[i, pl.ds(0, KINDS)], land.at[r, pl.ds(0, KINDS)], p_send.at[i], p_recv.at[r], group * RING + i, q
-        )
-
-    def half_copy(i):
-        return remote(half, full.at[q], q_send.at[i], q_recv.at[q], m, i)
-
-    goes = [[jnp.logical_not(to_self & (p % 4 == i) & (high == z)) for z in range(2)] for i in range(4)]
-
-    each(RING, r, lambda i: record_copy(i).start())
     each(COLUMN, y, lambda i: template_copy(i).start())
     ybuf[y] = msg[...]
+    local[3].wait()
     each(RING, r, lambda i: remote(xbuf.at[i], xbuf.at[i], x_send.at[i], x_recv.at[i], m, q).wait_recv())
 
     @pl.when(group > 0)
@@ -330,9 +356,9 @@
     each(COLUMN, y, lambda i: near_copy(i).start())
 
     each(COLUMN, y, lambda i: remote(msg, ybuf.at[i], w_send.at[i], w_recv.at[i], m, q).wait_recv())
-    for i in range(4):
-        for z in range(2):
-            pl.when(goes[i][z])(lambda i=i, z=z: pair_copy(i, z).start())
+    for z in range(2):
+        for i in range(4):
+            pl.when(goes[i][z] & (high >= z))(lambda i=i, z=z: pair_copy(i, z).start())
 
     @pl.when(to_self)
     def _():
@@ -343,7 +369,12 @@
         remote(xbuf.at[0], xbuf.at[RING], h_send, x_recv.at[RING], m, q).wait_recv()
 
     halo = xbuf[RING].astype(f32).reshape(ROWS, PIECE)
-    halo_sums(halo, run_ref, tail_ref)
+    after = halo_sums(halo, run_ref, tail_ref)
+
+    @pl.when(group == COLUMN - 1)
+    def _():
+        all_ref[COLUMN] = jnp.concatenate([after, jnp.zeros((7, 128), f32)], axis=0)
+
     x = jnp.concatenate([main, halo], axis=1)
     for j in range(SETS):
         shifted(j, x, h_ref)
@@ -353,7 +384,22 @@
         remote(block, block, s_send.at[i], s_recv.at[i], m, q).wait_recv()
 
     each(COLUMN, y, near)
-    far_copy().start()
+
+    @pl.when(low)
+    def _():
+        pl.semaphore_wait(ready, 5)
+        for i in range(4):
+            pair_copy(i, 1).start()
+        far_copy().start()
+
+
+    @pl.when(high == 1)
+    def _():
+        block = all_ref.at[pl.ds(0, COLUMN)]
+        remote(block, block, g_send, g_recv, m, q).wait_recv()
+
+    energy = window_energy(group, all_ref, run_ref, sum_ref, tail_ref, chain_ref, outer_ref, edge_ref, part_ref)
+    root_ref[...] = 1.0 / jnp.sqrt(energy + EPS)
 
     for cs in range(2):
         for k in range(KINDS):
@@ -369,28 +415,20 @@
     for j in range(SETS):
         correlate(j, h_ref, a_ref, z_ref, corr_ref)
 
-    far = all_ref.at[pl.ds(COLUMN * (1 - high), COLUMN)]
-    remote(far, far, g_send, g_recv, m, q).wait_recv()
-    energy = window_energy(group, all_ref, run_ref, sum_ref, tail_ref, chain_ref, outer_ref, edge_ref, part_ref)
-    total = stacked(1.0 / jnp.sqrt(energy + EPS), weight, sel, corr_ref, n_ref, z_ref)
+    total = stacked(root_ref[...], weight, sel, corr_ref, n_ref, z_ref)
     for i in range(RING):
-        part[i] = total[:, PIECE * i : PIECE * i + PIECE]
-
-    each(RING, r, lambda i: part_copy(i).start())
-    land[r, :KINDS] = part[r, :KINDS]
-    each(
-        RING, r,
-        lambda i: remote(
-            part.at[0, pl.ds(0, KINDS)], land.at[i, pl.ds(0, KINDS)], p_send.at[i], p_recv.at[i], m, q
-        ).wait_recv(),
-    )
-    half[...] = jnp.concatenate([jnp.sum(land[:, :KINDS], axis=0), jnp.zeros((KINDS, PIECE), f32)], axis=0)
-    each(KINDS, q, lambda i: half_copy(i).start())
-    full[q] = half[...]
-    each(KINDS, q, lambda i: remote(half, full.at[i], q_send.at[i], q_recv.at[i], m, q).wait_recv())
-    whole = jnp.sum(full[...], axis=0)
-    row = lax.broadcasted_iota(jnp.int32, (8, PIECE), 0)
-    out_ref[...] = jnp.sum(jnp.where(row == q, whole, 0.0), axis=0, keepdims=True)
+        for k in range(KINDS):
+            for c in range(PIECE // 128):
+                at = PIECE * i + 128 * c
+                part[KINDS * i + k, c : c + 1, :] = total[k : k + 1, at : at + 128]
+
+    me = KINDS * r + q
+    each(RING * KINDS, me, lambda i: part_copy(i).start())
+    land[me] = part[me]
+    each(RING * KINDS, me, lambda i: remote(part.at[0], land.at[i], p_send.at[i], p_recv.at[i], m, q).wait_recv())
+    whole = jnp.sum(land[...], axis=0)
+    for c in range(PIECE // 128):
+        out_ref[:, 128 * c : 128 * c + 128] = whole[c : c + 1]
 
     each(COLUMN, y, lambda i: template_copy(i).wait_send())
     each(RING, r, lambda i: record_copy(i).wait_send())
@@ -403,9 +441,12 @@
         for z in range(2):
             pl.when(goes[i][z])(lambda i=i, z=z: pair_copy(i, z).wait_send())
     each(COLUMN, y, lambda i: near_copy(i).wait_send())
-    far_copy().wait_send()
-    each(RING, r, lambda i: part_copy(i).wait_send())
-    each(KINDS, q, lambda i: half_copy(i).wait_send())
+
+    @pl.when(low)
+    def _():
+        far_copy().wait_send()
+
+    each(RING * KINDS, KINDS * r + q, lambda i: part_copy(i).wait_send())
 
 
 def local(records, templates, shifts, valid):
@@ -422,10 +463,8 @@
             pltpu.VMEM((COLUMN, 16, 256), bf16),
             pltpu.VMEM((16, 256), bf16),
             pltpu.VMEM((GROUPS, 8, 128), f32),
-            pltpu.VMEM((RING, 8, PIECE), f32),
-            pltpu.VMEM((RING, 8, PIECE), f32),
-            pltpu.VMEM((8, PIECE), f32),
-            pltpu.VMEM((KINDS, 8, PIECE), f32),
+            pltpu.VMEM((RING * KINDS, 8, 128), f32),
+            pltpu.VMEM((RING * KINDS, 8, 128), f32),
             pltpu.VMEM((1, OCT, L), bf16),
             pltpu.VMEM((2, 1, OCT), jnp.int32),
             pltpu.VMEM((SETS, 256, NH), bf16),
@@ -440,14 +479,15 @@
             pltpu.VMEM((256, 128), f32),
             pltpu.VMEM((256, 128), f32),
             pltpu.VMEM((128, 128), f32),
+            pltpu.VMEM((ROWS, NZ), f32),
             dma((COLUMN,)), dma((COLUMN,)),
             dma((8,)), dma((2 * KINDS,)),
             dma((RING,)), dma((RING + 1,)), dma,
             dma((COLUMN,)), dma((COLUMN,)),
             dma, dma,
-            dma((RING,)), dma((RING,)),
-            dma((KINDS,)), dma((KINDS,)),
+            dma((RING * KINDS,)), dma((RING * KINDS,)),
             dma((4,)),
+            pltpu.SemaphoreType.REGULAR,
         ],
         compiler_params=pltpu.CompilerParams(
             collective_id=0, has_side_effects=True, vmem_limit_bytes=63 * 1024 * 1024

time: 41.1 us -> 39.6 us (0.964)
  Pallas kernels: 39.7 us -> 38 us
    pallas_call x1, Pallas kernels: 39.7 us -> 38 us  [local(): pl.pallas_call(kernel, out_shape=jax.ShapeDtypeStruct((1, PIECE), f32), i...]
where the time goes in v2:
time: 39.6 us; the launch traced here: 39.2 us
  Pallas kernels  38 us (96%)
  local copies, waits for them, and re-layouts  1.24 us (3%)
    pallas_call x1, Pallas kernels, local(): pl.pallas_call(kernel, out_shape=jax.ShapeDtypeStruct((1, PIECE), f32), i...  38 us
    unnamed x1, local copies, waits for them, and re-layouts  1.24 us

profile of v2, /device:TPU:1, one launch (start us, length us, event | category | flops | bytes accessed | tf_op | source)
XLA Modules:
  0.0 39.2 jit_solution(12111579868637118710)
XLA Ops:
  0.0 38.0 %shard_map.46 = f32[1,384]{1,0:T(1,128)} custom-call(bf16[16,4,16,384]{3,2,1,0:T(8,128)(2,1)} %bitcast.1, bf16[1,8,300]{2,1,0:T(8,128)(2,1)} %tmpl_ref.1, s32[1,8]{1,0:T(1,128)} %shift_ref.1, s32[1,8]{1,0:T(1,128)} %valid_ref.1), custom_call_target="tpu_custom_call" | custom-call | tf_op jit(solution)/shard_map/pallas_call | solution.py:455
  38.0 1.2 %copy.6 = f32[1,384]{1,0:T(1,128)} copy(f32[1,384]{1,0:T(1,128)} %shard_map.46) | data formatting | bytes 3072

commit v3 on v2

--- a/solution.py
+++ b/solution.py
@@ -33,12 +33,12 @@
 bf16 = jnp.bfloat16
 
 
-def prepare(message, a_ref):
+def prepare(taps, a_ref):
     pairs = SETS * KINDS * OCT
-    low = message[:, :OCT, :].reshape(pairs, 256)
-    high = message[:, OCT:, :].reshape(pairs, 256)
-
-    parts = [low[:, :128].astype(bf16), low[:, 128:].astype(bf16), high[:, :128].astype(bf16)]
+    third = jnp.where(lax.broadcasted_iota(jnp.int32, (pairs, 128), 1) < L - 256, taps[:, 256:], 0.0)
+    thirds = [taps[:, :128], taps[:, 128:256], third]
+
+    parts = [part.astype(bf16) for part in thirds]
     lane = lax.broadcasted_iota(jnp.int32, (128, 256), 1)
     line = lax.broadcasted_iota(jnp.int32, (128, 256), 0)
     same = (lane % OCT) == (line % OCT)
@@ -50,10 +50,10 @@
             for j in range(SETS):
                 a_ref[j, 32 * u_lo : 32 * u_lo + 32, 256 * u_hi : 256 * u_hi + 256] = block[32 * j : 32 * j + 32]
 
-    shift = high[:, 128:129]
-    valid = high[:, 129:130]
+    shift = taps[:, L : L + 1]
+    valid = taps[:, L + 1 : L + 2]
     column = lax.broadcasted_iota(jnp.int32, (pairs, 128), 1)
-    squares = low[:, :128] ** 2 + low[:, 128:] ** 2 + high[:, :128] ** 2
+    squares = thirds[0] ** 2 + thirds[1] ** 2 + thirds[2] ** 2
     power = jnp.sum(squares, axis=1, keepdims=True) / L
     weight = valid / (L * jnp.sqrt(power + EPS))
 
@@ -76,13 +76,12 @@
     for n in range(NZ // 256):
         acc = None
         for u_hi in range(3):
-            rows = 64 if u_hi == 2 else 128
             part = jnp.dot(
-                a_ref[j, :rows, 256 * u_hi : 256 * u_hi + 256],
+                a_ref[j, :, 256 * u_hi : 256 * u_hi + 256],
                 h_ref[j, :, 256 * n + 128 * u_hi : 256 * n + 128 * u_hi + 256],
                 preferred_element_type=f32,
             )
-            acc = part if acc is None else jnp.concatenate([acc[:rows] + part, acc[rows:]], axis=0) if rows < 128 else acc + part
+            acc = part if acc is None else acc + part
         z_ref[slot, :, 256 * n : 256 * n + 256] = acc
     for k in range(KINDS):
         corr = z_ref[slot, 8 * k : 8 * k + 8, :]
@@ -205,7 +204,7 @@
 
 def kernel(
     rec_ref, tmpl_ref, shift_ref, valid_ref, out_ref,
-    xbuf, wbuf, ybuf, msg, all_ref, part, land, tbuf, ibuf,
+    xbuf, wbuf, ybuf, pair, msg, all_ref, part, land, tbuf, ibuf,
     h_ref, a_ref, z_ref, n_ref, corr_ref, run_ref, sum_ref, tail_ref, chain_ref, outer_ref, edge_ref, part_ref, root_ref,
     w_send, w_recv, f_send, f_recv, x_send, x_recv, h_send, s_send, s_recv, g_send, g_recv,
     p_send, p_recv, own, ready,
@@ -269,6 +268,19 @@
     def _():
         signal(m + RING, q)
 
+    for copy in local[:3]:
+        copy.wait()
+
+    waves = tbuf[0].astype(f32)
+    eye = lax.broadcasted_iota(jnp.int32, (OCT, OCT), 0) == lax.broadcasted_iota(jnp.int32, (OCT, OCT), 1)
+    moves = jnp.sum(jnp.where(eye, ibuf[0].astype(f32), 0.0), axis=1, keepdims=True)
+    masks = jnp.sum(jnp.where(eye, ibuf[1].astype(f32), 0.0), axis=1, keepdims=True)
+    lane = lax.broadcasted_iota(jnp.int32, (OCT, 128), 1)
+    tail = jnp.concatenate([waves[:, 256:], jnp.zeros((OCT, 128 - (L - 256)), f32)], axis=1)
+    tail = jnp.where(lane == L - 256, moves, jnp.where(lane == L - 255, masks, tail))
+    tail = jnp.concatenate([tail, jnp.zeros((OCT, 128), f32)], axis=1)
+    msg[...] = jnp.concatenate([waves[:, :256], tail], axis=0).astype(bf16)
+
     @pl.when(group == GROUPS - 1)
     def _():
         xbuf[RING] = jnp.zeros((2, ROWS // 2, PIECE), bf16)
@@ -306,7 +318,7 @@
 
     def pair_copy(i, z):
         return remote(
-            ybuf.at[pl.ds(2 * i, 2)], wbuf.at[KINDS * core + q], f_send.at[2 * i + z], f_recv.at[KINDS * core + q],
+            pair.at[i], wbuf.at[KINDS * core + q], f_send.at[2 * i + z], f_recv.at[KINDS * core + q],
             *pair_target(i, z),
         )
 
@@ -325,24 +337,14 @@
 
     def part_copy(i):
         me = KINDS * r + q
-        return remote(part.at[i], land.at[me], p_send.at[i], p_recv.at[me], group * RING + i // KINDS, i % KINDS)
+        return remote(
+            part.at[i, pl.ds(0, 3)], land.at[me, pl.ds(0, 3)], p_send.at[i], p_recv.at[me], group * RING + i // KINDS, i % KINDS
+        )
 
     goes = [[jnp.logical_not(to_self & (p % 4 == i) & (high == z)) for z in range(2)] for i in range(4)]
 
+    each(COLUMN, y, lambda i: template_copy(i).start())
     each(RING, r, lambda i: record_copy(i).start())
-    for copy in local[:3]:
-        copy.wait()
-
-    waves = tbuf[0].astype(f32)
-    eye = lax.broadcasted_iota(jnp.int32, (OCT, OCT), 0) == lax.broadcasted_iota(jnp.int32, (OCT, OCT), 1)
-    moves = jnp.sum(jnp.where(eye, ibuf[0].astype(f32), 0.0), axis=1, keepdims=True)
-    masks = jnp.sum(jnp.where(eye, ibuf[1].astype(f32), 0.0), axis=1, keepdims=True)
-    lane = lax.broadcasted_iota(jnp.int32, (OCT, 128), 1)
-    extra = jnp.where(lane == 0, moves, jnp.where(lane == 1, masks, 0.0))
-    tail = jnp.concatenate([waves[:, 256:], jnp.zeros((OCT, 128 - (L - 256)), f32)], axis=1)
-    msg[...] = jnp.concatenate([waves[:, :256], jnp.concatenate([tail, extra], axis=1)], axis=0).astype(bf16)
-
-    each(COLUMN, y, lambda i: template_copy(i).start())
     ybuf[y] = msg[...]
     local[3].wait()
     each(RING, r, lambda i: remote(xbuf.at[i], xbuf.at[i], x_send.at[i], x_recv.at[i], m, q).wait_recv())
@@ -356,13 +358,17 @@
     each(COLUMN, y, lambda i: near_copy(i).start())
 
     each(COLUMN, y, lambda i: remote(msg, ybuf.at[i], w_send.at[i], w_recv.at[i], m, q).wait_recv())
+    for i in range(4):
+        both = [ybuf[2 * i + e].astype(f32) for e in range(2)]
+        both = [jnp.concatenate([one[:OCT], one[OCT:, :128]], axis=1) for one in both]
+        pair[i] = jnp.concatenate(both, axis=0).astype(bf16)
     for z in range(2):
         for i in range(4):
             pl.when(goes[i][z] & (high >= z))(lambda i=i, z=z: pair_copy(i, z).start())
 
     @pl.when(to_self)
     def _():
-        wbuf[KINDS * core + q] = ybuf[pl.ds(2 * (p % 4), 2)]
+        wbuf[KINDS * core + q] = pair[p % 4]
 
     @pl.when(group < GROUPS - 1)
     def _():
@@ -410,7 +416,9 @@
                 ).wait_recv()
             )
     shards = wbuf[...].astype(f32)
-    shards = [shards[KINDS * cs + k, e : e + 1] for e in range(2) for cs in range(2) for k in range(KINDS)]
+    shards = [
+        shards[KINDS * cs + k, OCT * e : OCT * e + OCT] for e in range(2) for cs in range(2) for k in range(KINDS)
+    ]
     sel, weight = prepare(jnp.concatenate(shards, axis=0), a_ref)
     for j in range(SETS):
         correlate(j, h_ref, a_ref, z_ref, corr_ref)
@@ -424,9 +432,9 @@
 
     me = KINDS * r + q
     each(RING * KINDS, me, lambda i: part_copy(i).start())
-    land[me] = part[me]
-    each(RING * KINDS, me, lambda i: remote(part.at[0], land.at[i], p_send.at[i], p_recv.at[i], m, q).wait_recv())
-    whole = jnp.sum(land[...], axis=0)
+    land[me, :3] = part[me, :3]
+    each(RING * KINDS, me, lambda i: remote(part.at[0, pl.ds(0, 3)], land.at[i, pl.ds(0, 3)], p_send.at[i], p_recv.at[i], m, q).wait_recv())
+    whole = jnp.sum(land[:, :3], axis=0)
     for c in range(PIECE // 128):
         out_ref[:, 128 * c : 128 * c + 128] = whole[c : c + 1]
 
@@ -459,8 +467,9 @@
         out_specs=pl.BlockSpec(memory_space=pltpu.VMEM),
         scratch_shapes=[
             pltpu.VMEM((RING + 1, 2, ROWS // 2, PIECE), bf16),
-            pltpu.VMEM((2 * KINDS, 2, 16, 256), bf16),
+            pltpu.VMEM((2 * KINDS, 16, 384), bf16),
             pltpu.VMEM((COLUMN, 16, 256), bf16),
+            pltpu.VMEM((4, 16, 384), bf16),
             pltpu.VMEM((16, 256), bf16),
             pltpu.VMEM((GROUPS, 8, 128), f32),
             pltpu.VMEM((RING * KINDS, 8, 128), f32),

time: 39.6 us -> 38.4 us (0.970)
  the two profiles are of different devices: /device:TPU:1 before, /device:TPU:57 now
where the time goes in v3:
time: 38.4 us; the launch traced here: 38.2 us
  Pallas kernels  37 us (96%)
  local copies, waits for them, and re-layouts  1.24 us (3%)
    pallas_call x1, Pallas kernels, local(): pl.pallas_call(kernel, out_shape=jax.ShapeDtypeStruct((1, PIECE), f32), i...  37 us
    unnamed x1, local copies, waits for them, and re-layouts  1.24 us

profile of v3, /device:TPU:57, one launch (start us, length us, event | category | flops | bytes accessed | tf_op | source)
XLA Modules:
  0.0 38.2 jit_solution(2049139515715505487)
XLA Ops:
  0.0 37.0 %shard_map.46 = f32[1,384]{1,0:T(1,128)} custom-call(bf16[16,4,16,384]{3,2,1,0:T(8,128)(2,1)} %bitcast.1, bf16[1,8,300]{2,1,0:T(8,128)(2,1)} %tmpl_ref.1, s32[1,8]{1,0:T(1,128)} %shift_ref.1, s32[1,8]{1,0:T(1,128)} %valid_ref.1), custom_call_target="tpu_custom_call" | custom-call | tf_op jit(solution)/shard_map/pallas_call | solution.py:463
  37.0 1.2 %copy.6 = f32[1,384]{1,0:T(1,128)} copy(f32[1,384]{1,0:T(1,128)} %shard_map.46) | data formatting | bytes 3072

commit v4 on v3

--- a/solution.py
+++ b/solution.py
@@ -25,6 +25,7 @@
 NZ = 3328
 BIG = 3 * 256
 QUARTER = SPAN // 4
+EARLY = SPAN - 128
 LEVELS = 22
 BLOCKS = (WIDE // 16)
 CHAIN = 208
@@ -63,12 +64,14 @@
     return jnp.concatenate([sel, sel], axis=1)[: 4 * LEVELS], weight
 
 
-def shifted(j, x, h_ref):
-    x8 = jnp.concatenate([x[OCT * j : OCT * j + OCT], jnp.zeros((OCT, NH - WIDE), f32)], axis=1)
+def shifted(j, x, h_ref, start, keep):
+    x8 = x[OCT * j : OCT * j + OCT]
+    wide = x8.shape[1]
     for i in range(STEP // 2):
-        first = x8 if i == 0 else pltpu.roll(x8, NH - 2 * i, 1)
-        second = pltpu.roll(x8, NH - 2 * i - 1, 1)
-        h_ref[j, 16 * i : 16 * i + 16, :] = jnp.concatenate([first, second], axis=0).astype(bf16)
+        first = x8 if i == 0 else pltpu.roll(x8, wide - 2 * i, 1)
+        second = pltpu.roll(x8, wide - 2 * i - 1, 1)
+        both = jnp.concatenate([first[:, :keep], second[:, :keep]], axis=0)
+        h_ref[j, 16 * i : 16 * i + 16, start : start + keep] = both.astype(bf16)
 
 
 def correlate(j, h_ref, a_ref, z_ref, corr_ref):
@@ -206,7 +209,7 @@
     rec_ref, tmpl_ref, shift_ref, valid_ref, out_ref,
     xbuf, wbuf, ybuf, pair, msg, all_ref, part, land, tbuf, ibuf,
     h_ref, a_ref, z_ref, n_ref, corr_ref, run_ref, sum_ref, tail_ref, chain_ref, outer_ref, edge_ref, part_ref, root_ref,
-    w_send, w_recv, f_send, f_recv, x_send, x_recv, h_send, s_send, s_recv, g_send, g_recv,
+    w_send, w_recv, f_send, f_recv, x_send, x_recv, h_send, e_send, s_send, s_recv, g_send, g_recv,
     p_send, p_recv, own, ready,
 ):
     m, q = lax.axis_index("tm"), lax.axis_index("tmpl")
@@ -243,6 +246,8 @@
         copy.start()
 
     low = high == 0
+    passes = (group > 0) & (group != COLUMN)
+    head = m == COLUMN * RING
     other = (1 - high) * COLUMN * RING + y * RING + r
 
     def pair_target(i, z):
@@ -262,11 +267,12 @@
         for k in range(KINDS):
             source = ((p // 4) * COLUMN + y) * RING + 2 * x_at + cs
             pl.when(comes[cs][k] & (low | to_self))(functools.partial(signal, source, k))
-    each(RING * KINDS, KINDS * r + q, lambda i: signal(group * RING + i // KINDS, i % KINDS))
+    each(RING, r, lambda i: signal(group * RING + i, q))
+    each(KINDS, q, lambda i: signal(m, i))
 
     @pl.when(group < GROUPS - 1)
     def _():
-        signal(m + RING, q)
+        signal(jnp.where(group == COLUMN - 1, COLUMN * RING, m + RING), q)
 
     for copy in local[:3]:
         copy.wait()
@@ -287,7 +293,7 @@
 
     count = (
         (COLUMN - 1) + 4 - to_self.astype(jnp.int32)
-        + (RING * KINDS - 1) + (group > 0).astype(jnp.int32)
+        + (RING - 1) + (KINDS - 1) + passes.astype(jnp.int32) + RING * head.astype(jnp.int32)
         + high * (5 + 8 * (1 - to_self.astype(jnp.int32)))
     )
 
@@ -328,6 +334,9 @@
     def halo_copy():
         return remote(xbuf.at[0], xbuf.at[RING], h_send, x_recv.at[RING], m - RING, q)
 
+    def edge_copy(i):
+        return remote(record(i), xbuf.at[RING], e_send.at[i], x_recv.at[RING], (COLUMN - 1) * RING + i, q)
+
     def near_copy(i):
         return remote(all_ref.at[group], all_ref.at[group], s_send.at[i], s_recv.at[y], at_y(i), q)
 
@@ -344,12 +353,18 @@
     goes = [[jnp.logical_not(to_self & (p % 4 == i) & (high == z)) for z in range(2)] for i in range(4)]
 
     each(COLUMN, y, lambda i: template_copy(i).start())
+
+    @pl.when(head)
+    def _():
+        for i in range(RING):
+            edge_copy(i).start()
+
     each(RING, r, lambda i: record_copy(i).start())
     ybuf[y] = msg[...]
     local[3].wait()
     each(RING, r, lambda i: remote(xbuf.at[i], xbuf.at[i], x_send.at[i], x_recv.at[i], m, q).wait_recv())
 
-    @pl.when(group > 0)
+    @pl.when(passes)
     def _():
         halo_copy().start()
 
@@ -370,34 +385,39 @@
     def _():
         wbuf[KINDS * core + q] = pair[p % 4]
 
-    @pl.when(group < GROUPS - 1)
-    def _():
-        remote(xbuf.at[0], xbuf.at[RING], h_send, x_recv.at[RING], m, q).wait_recv()
-
-    halo = xbuf[RING].astype(f32).reshape(ROWS, PIECE)
-    after = halo_sums(halo, run_ref, tail_ref)
-
-    @pl.when(group == COLUMN - 1)
-    def _():
-        all_ref[COLUMN] = jnp.concatenate([after, jnp.zeros((7, 128), f32)], axis=0)
-
-    x = jnp.concatenate([main, halo], axis=1)
     for j in range(SETS):
-        shifted(j, x, h_ref)
+        shifted(j, main, h_ref, 0, EARLY)
 
     def near(i):
         block = all_ref.at[high * COLUMN + i]
         remote(block, block, s_send.at[i], s_recv.at[i], m, q).wait_recv()
 
-    each(COLUMN, y, near)
-
     @pl.when(low)
     def _():
+        each(COLUMN, y, near)
         pl.semaphore_wait(ready, 5)
         for i in range(4):
             pair_copy(i, 1).start()
         far_copy().start()
 
+    @pl.when(group < GROUPS - 1)
+    def _():
+        remote(xbuf.at[0], xbuf.at[RING], h_send, x_recv.at[RING], m, q).wait_recv()
+
+    halo = xbuf[RING].astype(f32).reshape(ROWS, PIECE)
+    after = halo_sums(halo, run_ref, tail_ref)
+
+    @pl.when(group == COLUMN - 1)
+    def _():
+        all_ref[COLUMN] = jnp.concatenate([after, jnp.zeros((7, 128), f32)], axis=0)
+
+    ending = jnp.concatenate([main[:, EARLY:], halo, jnp.zeros((ROWS, NH - WIDE), f32)], axis=1)
+    for j in range(SETS):
+        shifted(j, ending, h_ref, EARLY, NH - EARLY)
+
+    @pl.when(high == 1)
+    def _():
+        each(COLUMN, y, near)
 
     @pl.when(high == 1)
     def _():
@@ -441,9 +461,14 @@
     each(COLUMN, y, lambda i: template_copy(i).wait_send())
     each(RING, r, lambda i: record_copy(i).wait_send())
 
-    @pl.when(group > 0)
+    @pl.when(passes)
     def _():
         halo_copy().wait_send()
+
+    @pl.when(head)
+    def _():
+        for i in range(RING):
+            edge_copy(i).wait_send()
 
     for i in range(4):
         for z in range(2):
@@ -491,7 +516,7 @@
             pltpu.VMEM((ROWS, NZ), f32),
             dma((COLUMN,)), dma((COLUMN,)),
             dma((8,)), dma((2 * KINDS,)),
-            dma((RING,)), dma((RING + 1,)), dma,
+            dma((RING,)), dma((RING + 1,)), dma, dma((RING,)),
             dma((COLUMN,)), dma((COLUMN,)),
             dma, dma,
             dma((RING * KINDS,)), dma((RING * KINDS,)),

time: 38.4 us -> 37.8 us (0.984)
  the two profiles are of different devices: /device:TPU:57 before, /device:TPU:1 now
where the time goes in v4:
time: 37.8 us; the launch traced here: 37.7 us
  Pallas kernels  36.4 us (96%)
  local copies, waits for them, and re-layouts  1.24 us (3%)
    pallas_call x1, Pallas kernels, local(): pl.pallas_call(kernel, out_shape=jax.ShapeDtypeStruct((1, PIECE), f32), i...  36.4 us
    unnamed x1, local copies, waits for them, and re-layouts  1.24 us

profile of v4, /device:TPU:1, one launch (start us, length us, event | category | flops | bytes accessed | tf_op | source)
XLA Modules:
  0.0 37.7 jit_solution(718814718271243041)
XLA Ops:
  0.0 36.4 %shard_map.46 = f32[1,384]{1,0:T(1,128)} custom-call(bf16[16,4,16,384]{3,2,1,0:T(8,128)(2,1)} %bitcast.1, bf16[1,8,300]{2,1,0:T(8,128)(2,1)} %tmpl_ref.1, s32[1,8]{1,0:T(1,128)} %shift_ref.1, s32[1,8]{1,0:T(1,128)} %valid_ref.1), custom_call_target="tpu_custom_call" | custom-call | tf_op jit(solution)/shard_map/pallas_call | solution.py:488
  36.4 1.2 %copy.6 = f32[1,384]{1,0:T(1,128)} copy(f32[1,384]{1,0:T(1,128)} %shard_map.46) | data formatting | bytes 3072

commit v5 on v4

--- a/solution.py
+++ b/solution.py
@@ -362,15 +362,6 @@
     each(RING, r, lambda i: record_copy(i).start())
     ybuf[y] = msg[...]
     local[3].wait()
-    each(RING, r, lambda i: remote(xbuf.at[i], xbuf.at[i], x_send.at[i], x_recv.at[i], m, q).wait_recv())
-
-    @pl.when(passes)
-    def _():
-        halo_copy().start()
-
-    main = jnp.concatenate([xbuf[i].astype(f32).reshape(ROWS, PIECE) for i in range(RING)], axis=1)
-    all_ref[group] = block_sums(main, run_ref, sum_ref)
-    each(COLUMN, y, lambda i: near_copy(i).start())
 
     each(COLUMN, y, lambda i: remote(msg, ybuf.at[i], w_send.at[i], w_recv.at[i], m, q).wait_recv())
     for i in range(4):
@@ -384,6 +375,16 @@
     @pl.when(to_self)
     def _():
         wbuf[KINDS * core + q] = pair[p % 4]
+
+    each(RING, r, lambda i: remote(xbuf.at[i], xbuf.at[i], x_send.at[i], x_recv.at[i], m, q).wait_recv())
+
+    @pl.when(passes)
+    def _():
+        halo_copy().start()
+
+    main = jnp.concatenate([xbuf[i].astype(f32).reshape(ROWS, PIECE) for i in range(RING)], axis=1)
+    all_ref[group] = block_sums(main, run_ref, sum_ref)
+    each(COLUMN, y, lambda i: near_copy(i).start())
 
     for j in range(SETS):
         shifted(j, main, h_ref, 0, EARLY)

time: 37.8 us -> 36.7 us (0.971)
  Pallas kernels: 36.4 us -> 35.3 us
    pallas_call x1, Pallas kernels: 36.4 us -> 35.3 us  [local(): pl.pallas_call(kernel, out_shape=jax.ShapeDtypeStruct((1, PIECE), f32), i...]
where the time goes in v5:
time: 36.7 us; the launch traced here: 36.5 us
  Pallas kernels  35.3 us (96%)
  local copies, waits for them, and re-layouts  1.24 us (3%)
    pallas_call x1, Pallas kernels, local(): pl.pallas_call(kernel, out_shape=jax.ShapeDtypeStruct((1, PIECE), f32), i...  35.3 us
    unnamed x1, local copies, waits for them, and re-layouts  1.24 us

profile of v5, /device:TPU:1, one launch (start us, length us, event | category | flops | bytes accessed | tf_op | source)
XLA Modules:
  0.0 36.5 jit_solution(8124434221146390421)
XLA Ops:
  0.0 35.3 %shard_map.46 = f32[1,384]{1,0:T(1,128)} custom-call(bf16[16,4,16,384]{3,2,1,0:T(8,128)(2,1)} %bitcast.1, bf16[1,8,300]{2,1,0:T(8,128)(2,1)} %tmpl_ref.1, s32[1,8]{1,0:T(1,128)} %shift_ref.1, s32[1,8]{1,0:T(1,128)} %valid_ref.1), custom_call_target="tpu_custom_call" | custom-call | tf_op jit(solution)/shard_map/pallas_call | solution.py:489
  35.3 1.2 %copy.6 = f32[1,384]{1,0:T(1,128)} copy(f32[1,384]{1,0:T(1,128)} %shard_map.46) | data formatting | bytes 3072
